TPU v7x, 32 devices: a whole 2x2x4 slice. The times are simulated.
32 devices in a mesh: row: 4 (over y, core), col: 8 (over z, x).
Axes of the slice: x: 2, y: 2, z: 4, core: 2. Of those that a mesh axis runs over, the one named last changes fastest.
Arguments:
- tokens: bfloat16 [1024, 8192], P('col', 'row'), may hold values from -6 to 6
- query_weight: bfloat16 [8192, 8192], P('row', 'col'), may hold values from -0.0625 to 0.0625
- key_weight: bfloat16 [8192, 8192], P('row', 'col'), may hold values from -0.0625 to 0.0625
- value_weight: bfloat16 [8192, 8192], P('row', 'col'), may hold values from -0.0625 to 0.0625
- out_weight: bfloat16 [8192, 8192], P('col', 'row'), may hold values from -0.0625 to 0.0625
- filter_taps: float32 [7, 512], P(None, 'col'), may hold values from -4 to 4
- out_grad: bfloat16 [1024, 8192], P('col', 'row'), may hold values from -6 to 6
Outputs:
- block_out: bfloat16 [1024, 8192], P('col', 'row')
- tokens_grad: bfloat16 [1024, 8192], P('col', 'row')
- query_grad: bfloat16 [8192, 8192], P('row', 'col')
- key_grad: bfloat16 [8192, 8192], P('row', 'col')
- value_grad: bfloat16 [8192, 8192], P('row', 'col')
- outw_grad: bfloat16 [8192, 8192], P('col', 'row')
- taps_grad: float32 [7, 512], P(None, 'col')
All inputs are finite; a program needn't handle non-finite values.
Results may differ from a plain program's by a relative error of at most 0.035.
Values may be sent and summed in bfloat16 or wider, within the bound.
A program may use at most 128 MiB of HBM per device.

v0:
```python
import jax
import jax.numpy as jnp
from jax import lax
from jax.sharding import PartitionSpec as P

SEQS = 1
KW = 7
GROUP = 16


def from_behind(value, axis, by):
    length = lax.axis_size(axis)
    pairs = [(i, i + by) for i in range(length) if 0 <= i + by < length]
    return lax.ppermute(value, axis, pairs)


def contract_rows(left, right):
    return lax.dot_general(
        left, right, (((0,), (0,)), ((), ())), preferred_element_type=jnp.float32
    )


def contract_cols(left, right):
    return lax.dot_general(
        left, right, (((1,), (1,)), ((), ())), preferred_element_type=jnp.float32
    )


def forward_conv(before, channel_taps, positions, length):
    count_rows = positions.shape[0]
    lead = KW - 1
    total = jnp.zeros((count_rows, before.shape[1]), jnp.float32)
    for offset in range(KW):
        shifted = before[lead - offset : lead - offset + count_rows].astype(jnp.float32)
        keep = (positions % length >= offset)[:, None]
        total = total + jnp.where(keep, channel_taps[offset][None, :] * shifted, 0.0)
    return total


def backward_conv(after, channel_taps, positions, length):
    count_rows = positions.shape[0]
    total = jnp.zeros((count_rows, after.shape[1]), jnp.float32)
    for offset in range(KW):
        shifted = after[offset : offset + count_rows].astype(jnp.float32)
        keep = (positions % length + offset < length)[:, None]
        total = total + jnp.where(keep, channel_taps[offset][None, :] * shifted, 0.0)
    return total


def taps_partial(conv_grad, before, positions, length):
    count_rows = positions.shape[0]
    lead = KW - 1
    grad_wide = conv_grad.astype(jnp.float32)
    rows_grad = []
    for offset in range(KW):
        shifted = before[lead - offset : lead - offset + count_rows].astype(jnp.float32)
        keep = (positions % length >= offset)[:, None]
        rows_grad.append(jnp.sum(jnp.where(keep, grad_wide * shifted, 0.0), axis=0))
    stacked = jnp.stack(rows_grad)
    return stacked.reshape(KW, stacked.shape[1] // GROUP, GROUP).sum(axis=2)


def local(tokens, query_weight, key_weight, value_weight, out_weight, filter_taps, out_grad):
    row_count_axis = lax.axis_size("row")
    row_index = lax.axis_index("row")
    hidden_cols = query_weight.shape[1]
    full_tokens = lax.all_gather(tokens, "col", axis=0, tiled=True)
    total_tokens = full_tokens.shape[0]
    local_rows = total_tokens // row_count_axis
    length = total_tokens // SEQS
    taps_all = jnp.repeat(filter_taps, GROUP, axis=1)
    joined = jnp.concatenate([query_weight, key_weight, value_weight], axis=1)
    lead = KW - 1
    rows = full_tokens
    summed = lax.psum_scatter(
        jnp.dot(rows, joined, preferred_element_type=jnp.float32).astype(jnp.bfloat16),
        "row",
        scatter_dimension=0,
        tiled=True,
    )
    query = summed[:, :hidden_cols]
    keys = summed[:, hidden_cols : 2 * hidden_cols]
    values = summed[:, 2 * hidden_cols :]
    positions = row_index * local_rows + jnp.arange(local_rows, dtype=jnp.int32)
    product = (keys.astype(jnp.float32) * values.astype(jnp.float32)).astype(jnp.bfloat16)
    rim_before = from_behind(product[local_rows - lead :], "row", 1)
    before = jnp.concatenate([rim_before, product], axis=0)
    conv_out = forward_conv(before, taps_all, positions, length).astype(jnp.bfloat16)
    gated = (query.astype(jnp.float32) * conv_out.astype(jnp.float32)).astype(jnp.bfloat16)
    gated_all = lax.all_gather(gated, "row", axis=0, tiled=True)
    rows = gated_all
    block_out = lax.psum_scatter(
        jnp.dot(rows, out_weight, preferred_element_type=jnp.float32).astype(jnp.bfloat16),
        "col",
        scatter_dimension=0,
        tiled=True,
    )
    grad_all = lax.all_gather(out_grad, "col", axis=0, tiled=True)
    rows = grad_all
    gated_grad = lax.psum_scatter(
        contract_cols(rows, out_weight).astype(jnp.bfloat16), "row", scatter_dimension=0, tiled=True
    )
    query_back = (gated_grad.astype(jnp.float32) * conv_out.astype(jnp.float32)).astype(
        jnp.bfloat16
    )
    conv_grad = (gated_grad.astype(jnp.float32) * query.astype(jnp.float32)).astype(jnp.bfloat16)
    rim_after = from_behind(conv_grad[:lead], "row", -1)
    after = jnp.concatenate([conv_grad, rim_after], axis=0)
    product_grad = backward_conv(after, taps_all, positions, length)
    keys_back = (product_grad * values.astype(jnp.float32)).astype(jnp.bfloat16)
    values_back = (product_grad * keys.astype(jnp.float32)).astype(jnp.bfloat16)
    taps_term = taps_partial(conv_grad, before, positions, length)
    taps_grad = lax.psum(taps_term, "row")
    query_all, keys_all, values_all = (
        lax.all_gather(query_back, "row", axis=0, tiled=True),
        lax.all_gather(keys_back, "row", axis=0, tiled=True),
        lax.all_gather(values_back, "row", axis=0, tiled=True),
    )
    query_grad = contract_rows(full_tokens, query_all).astype(jnp.bfloat16)
    key_grad = contract_rows(full_tokens, keys_all).astype(jnp.bfloat16)
    value_grad = contract_rows(full_tokens, values_all).astype(jnp.bfloat16)
    outw_grad = contract_rows(gated_all, grad_all).astype(jnp.bfloat16)
    tokens_grad = lax.psum_scatter(
        (
            contract_cols(query_all, query_weight)
            + contract_cols(keys_all, key_weight)
            + contract_cols(values_all, value_weight)
        ).astype(jnp.bfloat16),
        "col",
        scatter_dimension=0,
        tiled=True,
    )
    return (block_out, tokens_grad, query_grad, key_grad, value_grad, outw_grad, taps_grad)


def solution(mesh):
    in_specs = (
        P("col", "row"),
        P("row", "col"),
        P("row", "col"),
        P("row", "col"),
        P("col", "row"),
        P(None, "col"),
        P("col", "row"),
    )
    out_specs = (
        P("col", "row"),
        P("col", "row"),
        P("row", "col"),
        P("row", "col"),
        P("row", "col"),
        P("col", "row"),
        P(None, "col"),
    )
    return jax.shard_map(local, mesh=mesh, in_specs=in_specs, out_specs=out_specs, check_vma=False)
```

profile of v0, /device:TPU:0, one launch (start us, length us, event | category | flops | bytes accessed | tf_op | source)
XLA Modules:
  0.0 549.5 jit_solution(7688224694278276150)
XLA Ops:
  8.7 77.6 %all-gather.7.cloned.1.call-done = bf16[1024,2048]{1,0:T(8,128)(2,1)} async-done(((bf16[128,2048]{1,0:T(8,128)(2,1)}), bf16[1024,2048]{1,0:T(8,128)(2,1)}) %all-gather.7.cloned.1.call-update) | async-done | bytes 4194320 | tf_op jit(solution)/shard_map/all_gather | solution.py:67
  86.3 20.4 %convert_bitcast_fusion = bf16[1024,3072]{0,1:T(8,128)(2,1)} fusion(bf16[1024,2048]{1,0:T(8,128)(2,1)} %all-gather.7.cloned.1.call-done, bf16[2048,1024]{1,0:T(8,128)(2,1)} %param.10, bf16[2048,1024]{1,0:T(8,128)(2,1)} %param.9, bf16[2048,1024]{1,0:T(8,128)(2,1)} %param.8), kind=kOutput, calls=%fused_computation.7 | convolution fusion | flops 12925796352 | bytes 23068672 | tf_op jit(solution)/shard_map/dot_general | solution.py:76
  106.7 53.3 %all-gather.11.cloned.1.call-done = bf16[1024,2048]{1,0:T(8,128)(2,1)} async-done(((bf16[128,2048]{1,0:T(8,128)(2,1)}), bf16[1024,2048]{1,0:T(8,128)(2,1)}) %all-gather.11.cloned.1.call-update) | async-done | bytes 4194320 | tf_op jit(solution)/shard_map/all_gather | solution.py:98
  160.1 9.3 %convolution_convert_fusion.2 = bf16[1024,1024]{0,1:T(8,128)(2,1)} fusion(bf16[1024,2048]{1,0:T(8,128)(2,1)} %all-gather.11.cloned.1.call-done, bf16[1024,2048]{1,0:T(8,128)(2,1)} %param.11), kind=kOutput, calls=%fused_computation.21 | convolution fusion | flops 4296015872 | bytes 10485760 | tf_op jit(solution)/shard_map/dot_general | solution.py:24
  169.5 49.7 %reduce-scatter.5.cloned.1.call-done = bf16[256,3072]{0,1:T(8,128)(2,1)} async-done(((bf16[1024,3072]{0,1:T(8,128)(2,1)}), bf16[256,3072]{0,1:T(8,128)(2,1)}) %reduce-scatter.5.cloned.1.call-update) | async-done | bytes 1572880 | tf_op jit(solution)/shard_map/reduce_scatter | solution.py:75
  223.7 30.1 %reduce-scatter.9.cloned.1.call-done = bf16[256,1024]{0,1:T(8,128)(2,1)} async-done(((bf16[1024,1024]{0,1:T(8,128)(2,1)}), bf16[256,1024]{0,1:T(8,128)(2,1)}) %reduce-scatter.9.cloned.1.call-update) | async-done | bytes 524304 | tf_op jit(solution)/shard_map/reduce_scatter | solution.py:100
  272.2 10.5 %all-gather.13.cloned.1.call-done = bf16[1024,1024]{0,1:T(8,128)(2,1)} async-done(((bf16[256,1024]{0,1:T(8,128)(2,1)}), bf16[1024,1024]{0,1:T(8,128)(2,1)}) %all-gather.13.cloned.1.call-update) | async-done | bytes 2097168 | tf_op jit(solution)/shard_map/all_gather | solution.py:115
  282.7 10.7 %fusion.64 = f32[1024,2048]{1,0:T(8,128)} fusion(bf16[1024,1024]{0,1:T(8,128)(2,1)} %all-gather.13.cloned.1.call-done, bf16[2048,1024]{1,0:T(8,128)(2,1)} %param.8), kind=kOutput, calls=%fused_computation.141 | convolution fusion | flops 4294967296 | bytes 14680064 | tf_op jit(solution)/shard_map/dot_general | solution.py:24
  293.4 14.2 %all-gather.15.cloned.1.call-done = bf16[1024,1024]{0,1:T(8,128)(2,1)} async-done(((bf16[256,1024]{0,1:T(8,128)(2,1)}), bf16[1024,1024]{0,1:T(8,128)(2,1)}) %all-gather.15.cloned.1.call-update) | async-done | bytes 2097168 | tf_op jit(solution)/shard_map/all_gather | solution.py:116
  307.6 10.7 %fusion.65 = f32[1024,2048]{1,0:T(8,128)} fusion(bf16[1024,1024]{0,1:T(8,128)(2,1)} %all-gather.15.cloned.1.call-done, bf16[2048,1024]{1,0:T(8,128)(2,1)} %param.9), kind=kOutput, calls=%fused_computation.142 | convolution fusion | flops 4294967296 | bytes 14680064 | tf_op jit(solution)/shard_map/dot_general | solution.py:24
  318.3 14.3 %all-gather.17.cloned.1.call-done = bf16[1024,1024]{0,1:T(8,128)(2,1)} async-done(((bf16[256,1024]{0,1:T(8,128)(2,1)}), bf16[1024,1024]{0,1:T(8,128)(2,1)}) %all-gather.17.cloned.1.call-update) | async-done | bytes 2097168 | tf_op jit(solution)/shard_map/all_gather | solution.py:117
  332.6 14.4 %add_convert_fusion = bf16[1024,2048]{1,0:T(8,128)(2,1)} fusion(f32[1024,2048]{1,0:T(8,128)} %fusion.64, f32[1024,2048]{1,0:T(8,128)} %fusion.65, bf16[1024,1024]{0,1:T(8,128)(2,1)} %all-gather.17.cloned.1.call-done, bf16[2048,1024]{1,0:T(8,128)(2,1)} %param.10), kind=kOutput, calls=%fused_computation.6 | convolution fusion | flops 4301258752 | bytes 27262976 | tf_op jit(solution)/shard_map/dot_general | solution.py:24
  347.1 10.5 %all-gather.9.cloned.1.call-done = bf16[1024,1024]{0,1:T(8,128)(2,1)} async-done(((bf16[256,1024]{0,1:T(8,128)(2,1)}), bf16[1024,1024]{0,1:T(8,128)(2,1)}) %all-gather.9.cloned.1.call-update) | async-done | bytes 2097168 | tf_op jit(solution)/shard_map/all_gather | solution.py:90
  357.6 9.3 %convolution_convert_fusion.1 = bf16[1024,2048]{1,0:T(8,128)(2,1)} fusion(bf16[1024,1024]{0,1:T(8,128)(2,1)} %all-gather.9.cloned.1.call-done, bf16[1024,2048]{1,0:T(8,128)(2,1)} %param.11), kind=kOutput, calls=%fused_computation.12 | convolution fusion | flops 4297064448 | bytes 10485760 | tf_op jit(solution)/shard_map/dot_general | solution.py:93
  368.4 7.2 %psum.7 = f32[7,64]{1,0:T(8,128)} all-reduce(f32[7,64]{1,0:T(8,128)S(1)} %reduce_sum.79), channel_id=1, replica_groups=mesh['row'=4,'col'=8] {'row'}, use_global_device_ids=true, to_apply=%region_12.13 | all-reduce | flops 448 | bytes 3584 | tf_op jit(solution)/shard_map/psum | solution.py:113
  375.6 9.4 %convert_bitcast_fusion.3 = bf16[2048,1024]{0,1:T(8,128)(2,1)} fusion(bf16[1024,1024]{0,1:T(8,128)(2,1)} %all-gather.13.cloned.1.call-done, bf16[1024,2048]{1,0:T(8,128)(2,1)} %all-gather.7.cloned.1.call-done), kind=kOutput, calls=%fused_computation.10 | convolution fusion | flops 4297064448 | bytes 10485760 | tf_op jit(solution)/shard_map/dot_general | solution.py:18
  384.9 6.6 %copy.30 = bf16[2048,1024]{1,0:T(8,128)(2,1)} copy(bf16[2048,1024]{0,1:T(8,128)(2,1)} %convert_bitcast_fusion.3) | data formatting | bytes 8388608
  391.5 8.2 %convert_bitcast_fusion.2 = bf16[2048,1024]{0,1:T(8,128)(2,1)} fusion(bf16[1024,1024]{0,1:T(8,128)(2,1)S(1)} %copy-done.2, bf16[1024,2048]{1,0:T(8,128)(2,1)} %all-gather.7.cloned.1.call-done), kind=kOutput, calls=%fused_computation.9 | convolution fusion | flops 4297064448 | bytes 10485760 | tf_op jit(solution)/shard_map/dot_general | solution.py:18
  399.8 6.6 %copy.31 = bf16[2048,1024]{1,0:T(8,128)(2,1)} copy(bf16[2048,1024]{0,1:T(8,128)(2,1)} %convert_bitcast_fusion.2) | data formatting | bytes 8388608
  406.3 8.2 %convert_bitcast_fusion.1 = bf16[2048,1024]{0,1:T(8,128)(2,1)} fusion(bf16[1024,1024]{0,1:T(8,128)(2,1)S(1)} %copy-done.3, bf16[1024,2048]{1,0:T(8,128)(2,1)} %all-gather.7.cloned.1.call-done), kind=kOutput, calls=%fused_computation.8 | convolution fusion | flops 4297064448 | bytes 10485760 | tf_op jit(solution)/shard_map/dot_general | solution.py:18
  414.5 6.6 %copy.32 = bf16[2048,1024]{1,0:T(8,128)(2,1)} copy(bf16[2048,1024]{0,1:T(8,128)(2,1)} %convert_bitcast_fusion.1) | data formatting | bytes 8388608
  421.1 8.3 %convolution_convert_fusion = bf16[1024,2048]{1,0:T(8,128)(2,1)} fusion(bf16[1024,1024]{0,1:T(8,128)(2,1)S(1)} %copy-done.4, bf16[1024,2048]{1,0:T(8,128)(2,1)} %all-gather.11.cloned.1.call-done), kind=kOutput, calls=%fused_computation.11 | convolution fusion | flops 4297064448 | bytes 10485760 | tf_op jit(solution)/shard_map/dot_general | solution.py:18
  429.4 20.6 %reduce-scatter.11.cloned.1.call-done = bf16[128,2048]{1,0:T(8,128)(2,1)} async-done(((bf16[1024,2048]{1,0:T(8,128)(2,1)}), bf16[128,2048]{1,0:T(8,128)(2,1)}) %reduce-scatter.11.cloned.1.call-update) | async-done | bytes 524304 | tf_op jit(solution)/shard_map/reduce_scatter | solution.py:123
  449.9 92.3 %reduce-scatter.7.cloned.1.call-done = bf16[128,2048]{1,0:T(8,128)(2,1)} async-done(((bf16[1024,2048]{1,0:T(8,128)(2,1)}), bf16[128,2048]{1,0:T(8,128)(2,1)}) %reduce-scatter.7.cloned.1.call-update) | async-done | bytes 524304 | tf_op jit(solution)/shard_map/reduce_scatter | solution.py:92
  (87 shorter events, 25.9 us)
Async XLA Ops:
  7.2 79.1 %all-gather.7.cloned.1.call-start = ((), (), s32[]{:S(2)}) async-start(), calls=%async_computation.4 | async-start | bytes 4718592 | tf_op jit(solution)/shard_map/all_gather | solution.py:67
  7.9 152.2 %all-gather.11.cloned.1.call-start = ((), (), s32[]{:S(2)}) async-start(), calls=%async_computation.8 | async-start | bytes 4718592 | tf_op jit(solution)/shard_map/all_gather | solution.py:98
  8.7 210.6 %reduce-scatter.5.cloned.1.call-start = ((), (), s32[]{:S(2)}) async-start(), calls=%async_computation.5 | async-start | bytes 7864320 | tf_op jit(solution)/shard_map/reduce_scatter | solution.py:75
  106.7 62.8 %copy-start.1 = (f32[7,64]{1,0:T(8,128)S(1)}, f32[7,64]{1,0:T(8,128)}, u32[]{:S(2)}) copy-start(f32[7,64]{1,0:T(8,128)} %param.12) | copy-start | bytes 5380
  106.7 147.2 %reduce-scatter.9.cloned.1.call-start = ((), (), s32[]{:S(2)}) async-start(), calls=%async_computation.9 | async-start | bytes 2621440 | tf_op jit(solution)/shard_map/reduce_scatter | solution.py:100
  169.4 113.3 %all-gather.13.cloned.1.call-start = ((), (), s32[]{:S(2)}) async-start(), calls=%async_computation.10 | async-start | bytes 2621440 | tf_op jit(solution)/shard_map/all_gather | solution.py:115
  219.3 39.3 %copy-start = (bf16[256,3072]{0,1:T(8,128)(2,1)S(1)}, bf16[256,3072]{0,1:T(8,128)(2,1)}, u32[]{:S(2)}) copy-start(bf16[256,3072]{0,1:T(8,128)(2,1)} %reduce-scatter.5.cloned.1.call-done) | copy-start | bytes 4718596
  220.9 33.0 %collective-permute-start = (bf16[6,1024]{0,1:T(8,128)(2,1)S(1)}, bf16[6,1024]{0,1:T(8,128)(2,1)S(1)}, u32[]{:S(2)}, u32[]{:S(2)}) collective-permute-start(bf16[6,1024]{0,1:T(8,128)(2,1)S(1)} %slice.147), channel_id=1, source_target_pairs={{0,8},{8,16},{16,24},{1,9},{9,17},{17,25},{2,10},{10,18},{18,26},{... | collective-permute-start | bytes 36872 | tf_op jit(solution)/shard_map/ppermute | solution.py:14
  258.5 49.1 %all-gather.15.cloned.1.call-start = ((), (), s32[]{:S(2)}) async-start(), calls=%async_computation.11 | async-start | bytes 2621440 | tf_op jit(solution)/shard_map/all_gather | solution.py:116
  262.0 3.4 collective-permute-start.1
  270.5 62.1 %all-gather.17.cloned.1.call-start = ((), (), s32[]{:S(2)}) async-start(), calls=%async_computation.12 | async-start | bytes 2621440 | tf_op jit(solution)/shard_map/all_gather | solution.py:117
  271.3 86.3 %all-gather.9.cloned.1.call-start = ((), (), s32[]{:S(2)}) async-start(), calls=%async_computation.6 | async-start | bytes 2621440 | tf_op jit(solution)/shard_map/all_gather | solution.py:90
  272.0 177.9 %reduce-scatter.11.cloned.1.call-start = ((), (), s32[]{:S(2)}) async-start(), calls=%async_computation.13 | async-start | bytes 4718592 | tf_op jit(solution)/shard_map/reduce_scatter | solution.py:123
  347.0 195.2 %reduce-scatter.7.cloned.1.call-start = ((), (), s32[]{:S(2)}) async-start(), calls=%async_computation.7 | async-start | bytes 4718592 | tf_op jit(solution)/shard_map/reduce_scatter | solution.py:92
  384.9 6.6 %copy-start.2 = (bf16[1024,1024]{0,1:T(8,128)(2,1)S(1)}, bf16[1024,1024]{0,1:T(8,128)(2,1)}, u32[]{:S(2)}) copy-start(bf16[1024,1024]{0,1:T(8,128)(2,1)} %all-gather.15.cloned.1.call-done) | copy-start | bytes 6291460
  399.7 6.6 %copy-start.3 = (bf16[1024,1024]{0,1:T(8,128)(2,1)S(1)}, bf16[1024,1024]{0,1:T(8,128)(2,1)}, u32[]{:S(2)}) copy-start(bf16[1024,1024]{0,1:T(8,128)(2,1)} %all-gather.17.cloned.1.call-done) | copy-start | bytes 6291460
  414.5 6.6 %copy-start.4 = (bf16[1024,1024]{0,1:T(8,128)(2,1)S(1)}, bf16[1024,1024]{0,1:T(8,128)(2,1)}, u32[]{:S(2)}) copy-start(bf16[1024,1024]{0,1:T(8,128)(2,1)} %all-gather.9.cloned.1.call-done) | copy-start | bytes 6291460
Sparse Core Ops, SparseCore 0:
  10.1 76.0 all-gather.6
  88.4 71.6 all-gather.10
  162.6 56.6 reduce-scatter.4
  222.4 31.4 reduce-scatter.8
  258.6 24.0 all-gather.12
  284.7 22.8 all-gather.14
  309.7 22.8 all-gather.16
  334.7 22.8 all-gather.8
  361.8 88.0 reduce-scatter.10
  454.4 87.8 reduce-scatter.6
where the time goes:
time: 559 us; the launch traced here: 550 us
  waiting for transfers between devices  378 us (68%)
  matrix products  109 us (19%)
  local copies, waits for them, and re-layouts  22.1 us (4%)
  other arithmetic  14.9 us (3%)
  between operations  14.8 us (3%)
  blocking collectives  7.16 us (1%)
    reduce_scatter x1, waiting for transfers between devices, local(): lax.psum_scatter(jnp.dot(rows, out_weight, preferred_element_type=jnp.flo...  92.3 us
    all_gather x1, waiting for transfers between devices, local(): full_tokens = lax.all_gather(tokens, 'col', axis=0, tiled=True)  77.6 us
    all_gather x1, waiting for transfers between devices, local(): grad_all = lax.all_gather(out_grad, 'col', axis=0, tiled=True)  53.3 us
    reduce_scatter x1, waiting for transfers between devices, local(): lax.psum_scatter(jnp.dot(rows, joined, preferred_element_type=jnp.float32...  49.7 us
    dot_general x4, matrix products, contract_cols(): lax.dot_general(left, right, (((1,), (1,)), ((), ())), preferred_element_...  45.1 us
    dot_general x4, matrix products, contract_rows(): lax.dot_general(left, right, (((0,), (0,)), ((), ())), preferred_element_...  34 us
    reduce_scatter x1, waiting for transfers between devices, local(): lax.psum_scatter(contract_cols(rows, out_weight).astype(jnp.bfloat16), 'r...  30.1 us
    reduce_scatter x1, waiting for transfers between devices, local(): lax.psum_scatter((contract_cols(query_all, query_weight) + contract_cols(...  20.6 us
  transfers between devices with their start and end apart: 12, of which 11 were waited for; matrix products, arithmetic and copies ran while one was open for 26% of the time, Pallas kernels for 0%

commit v1 on v0

v1 whole, which is shorter than its diff:
```python
import functools

import jax
import jax.numpy as jnp
from jax import lax
from jax.experimental import pallas as pl
from jax.experimental.pallas import tpu as pltpu
from jax.sharding import PartitionSpec as P

SEQS = 1
KW = 7
GROUP = 16
Z_LINE = 4
CORES = 2
WIDE = 512
MESH = pl.DeviceIdType.MESH
VMEM_BYTES = 62 * 1024 * 1024


def contract_rows(left, right):
    return lax.dot_general(
        left, right, (((0,), (0,)), ((), ())), preferred_element_type=jnp.float32
    )


def contract_cols(left, right):
    return lax.dot_general(
        left, right, (((1,), (1,)), ((), ())), preferred_element_type=jnp.float32
    )


def push(src, dst, send, recv, axis, index):
    return pltpu.make_async_remote_copy(
        src_ref=src,
        dst_ref=dst,
        send_sem=send,
        recv_sem=recv,
        device_id={axis: index},
        device_id_type=MESH,
    )


def greet(n_col, n_row):
    col, row = lax.axis_index("col"), lax.axis_index("row")
    barrier = pltpu.get_barrier_semaphore()
    for i in range(1, n_col):
        pl.semaphore_signal(
            barrier, inc=1, device_id={"col": lax.rem(col + i, n_col)}, device_id_type=MESH
        )
    for i in range(1, n_row):
        pl.semaphore_signal(
            barrier, inc=1, device_id={"row": lax.rem(row + i, n_row)}, device_id_type=MESH
        )
    pl.semaphore_wait(barrier, n_col + n_row - 2)


def forward_kernel(
    n_col, n_row, n_z,
    tokens, grads, wq, wk, wv, wo,
    sums, tokens_all, grads_all,
    held, w_in, w_out, parts, got,
    z_send, z_recv, x_send, x_recv, r_send, r_recv, w_sem, own_sem, out_sem,
):
    n_x = n_col // n_z
    col, me = lax.axis_index("col"), lax.axis_index("row")
    z, x = col // n_x, lax.rem(col, n_x)
    hidden = w_in.shape[2]
    slice_cols = hidden // n_row
    own_copies = [
        pltpu.make_async_copy(ref, held.at[a, col], own_sem.at[a])
        for a, ref in enumerate((tokens, grads))
    ]
    for copy in own_copies:
        copy.start()
    weight_copies = [
        pltpu.make_async_copy(ref, w_in.at[m], w_sem.at[m]) for m, ref in enumerate((wq, wk, wv))
    ] + [pltpu.make_async_copy(wo, w_out, w_sem.at[3])]
    for copy in weight_copies:
        copy.start()
    greet(n_col, n_row)
    own_copies[0].wait()
    own_copies[1].wait()

    def z_copy(a, block, way):
        slot = held.at[a, block * n_x + x]
        return push(slot, slot, z_send.at[a, way, block], z_recv.at[a, block], "col",
                    (z + 1 - 2 * way) * n_x + x)

    def x_copy(a, block, source, i):
        slot = held.at[a, block * n_x + source]
        return push(slot, slot, x_send.at[a, block, i], x_recv.at[a, block, source], "col",
                    z * n_x + lax.rem(x + i, n_x))

    def out_copy(a, block):
        dst = (tokens_all, grads_all)[a]
        return pltpu.make_async_copy(held.at[a, block], dst.at[block], out_sem.at[a, block])

    def r_copy(a, block, to, source):
        which = pl.ds(0, 3) if a == 0 else pl.ds(3, 1)
        return push(parts.at[to, block, which], got.at[source, block, which],
                    r_send.at[a, to, block], r_recv.at[a, source, block], "row", to)

    def work(a, block):
        out_copy(a, block).start()

        def one(m, carry):
            rows = held[a, block]
            if a == 0:
                part = jnp.dot(rows, w_in[m], preferred_element_type=jnp.float32)
            else:
                part = contract_cols(rows, w_out[...])
            part = part.astype(jnp.bfloat16)
            for to in range(n_row):
                parts[to, block, m if a == 0 else 3] = part[:, to * slice_cols:(to + 1) * slice_cols]
            return carry

        if a == 0:
            lax.fori_loop(0, 3, one, 0)
        else:
            one(3, 0)
        for i in range(1, n_row):
            r_copy(a, block, lax.rem(me + i, n_row), me).start()

    def arrived(a, block):
        for i in range(1, n_x):
            x_copy(a, block, x, i).start()
        work(a, block * n_x + x)

        def other(i, carry):
            source = lax.rem(x + i, n_x)
            x_copy(a, block, source, 1).wait_recv()
            work(a, block * n_x + source)
            return carry

        lax.fori_loop(1, n_x, other, 0)

    for a in range(2):
        @pl.when(z + 1 < n_z)
        def _():
            z_copy(a, z, 0).start()

        @pl.when(z > 0)
        def _():
            z_copy(a, z, 1).start()

        if a == 0:
            for copy in weight_copies[:3]:
                copy.wait()
        else:
            weight_copies[3].wait()
        arrived(a, z)

        def step(s, carry):
            before, after = z - s, z + s

            @pl.when(before >= 0)
            def _():
                z_copy(a, before, 0).wait_recv()

                @pl.when(z + 1 < n_z)
                def _():
                    z_copy(a, before, 0).start()

            @pl.when(after < n_z)
            def _():
                z_copy(a, after, 1).wait_recv()

                @pl.when(z > 0)
                def _():
                    z_copy(a, after, 1).start()

            @pl.when(before >= 0)
            def _():
                arrived(a, before)

            @pl.when(after < n_z)
            def _():
                arrived(a, after)

            return carry

        lax.fori_loop(1, n_z, step, 0)

    def total(block, carry):
        for a, which in ((0, range(3)), (1, range(3, 4))):
            for i in range(1, n_row):
                r_copy(a, block, me, lax.rem(me + i, n_row)).wait_recv()
            for m in which:
                value = parts[me, block, m].astype(jnp.float32)
                for i in range(1, n_row):
                    value = value + got[lax.rem(me + i, n_row), block, m].astype(jnp.float32)
                sums[m, block] = value.astype(jnp.bfloat16)
        return carry

    lax.fori_loop(0, n_col, total, 0)

    for a in range(2):
        def finish_z(block, carry):
            @pl.when((block <= z) & (z + 1 < n_z))
            def _():
                z_copy(a, block, 0).wait_send()

            @pl.when((block >= z) & (z > 0))
            def _():
                z_copy(a, block, 1).wait_send()

            for i in range(1, n_x):
                x_copy(a, block, x, i).wait_send()
            return carry

        lax.fori_loop(0, n_z, finish_z, 0)

        def finish_block(block, carry):
            out_copy(a, block).wait()
            for i in range(1, n_row):
                r_copy(a, block, lax.rem(me + i, n_row), me).wait_send()
            return carry

        lax.fori_loop(0, n_col, finish_block, 0)


def backward_kernel(
    n_col, n_row, n_z,
    acts, wo, wq, wk, wv,
    block_out, tokens_grad, acts_all,
    held, w_out, w_in, parts, x_got, z_got,
    w_sem, own_sem, g_send, g_recv, x_send, x_recv, z_send, z_recv, out_sem,
):
    n_x, n_y = n_col // n_z, n_row // CORES
    col, me = lax.axis_index("col"), lax.axis_index("row")
    z, x = col // n_x, lax.rem(col, n_x)
    y, core = me // CORES, lax.rem(me, CORES)
    partner = y * CORES + 1 - core
    block_rows = parts.shape[2]
    features = parts.shape[3]
    own_copies = [
        pltpu.make_async_copy(acts.at[m], held.at[m, me], own_sem.at[m]) for m in range(4)
    ]
    for copy in own_copies:
        copy.start()
    weight_copies = [pltpu.make_async_copy(wo, w_out, w_sem.at[0])] + [
        pltpu.make_async_copy(ref, w_in.at[m], w_sem.at[m + 1]) for m, ref in enumerate((wq, wk, wv))
    ]
    for copy in weight_copies:
        copy.start()
    greet(n_col, n_row)

    def g_copy(m, source, slot, to):
        return push(held.at[m, source], held.at[m, source], g_send.at[m, slot],
                    g_recv.at[m, source], "row", to)

    def out_copy(m, source):
        return pltpu.make_async_copy(held.at[m, source], acts_all.at[m, source], out_sem.at[m, source])

    for m in range(4):
        own_copies[m].wait()
        for i in range(1, n_y):
            g_copy(m, me, i, lax.rem(y + i, n_y) * CORES + core).start()
        g_copy(m, me, 0, partner).start()

    def pass_on(m):
        out_copy(m, me).start()
        for i in range(1, n_y):
            source = lax.rem(y + i, n_y) * CORES + core
            g_copy(m, source, 0, partner).wait_recv()
            g_copy(m, source, n_y - 1 + i, partner).start()
            out_copy(m, source).start()

    def settle(m):
        for i in range(n_y):
            source = lax.rem(y + i, n_y) * CORES + 1 - core
            g_copy(m, source, 0, partner).wait_recv()
            out_copy(m, source).start()

    def act(m, block):
        rows = pl.ds(pl.multiple_of(block * block_rows, block_rows), block_rows)
        return jnp.concatenate([held[m, r, rows] for r in range(n_row)], axis=1)

    def x_copy(phase, block, to, source):
        return push(parts.at[phase, block * n_x + to], x_got.at[phase, source, block],
                    x_send.at[phase, block, to], x_recv.at[phase, source, block], "col",
                    z * n_x + to)

    def z_copy(phase, block, way):
        return push(parts.at[phase, block * n_x + x], z_got.at[phase, way, block],
                    z_send.at[phase, block], z_recv.at[phase, way, block], "col",
                    (z + 1 - 2 * way) * n_x + x)

    def multiply(phase, block):
        wide = min(WIDE, features)

        def tile(n, carry):
            cols = pl.ds(pl.multiple_of(n * wide, wide), wide)
            if phase == 0:
                value = jnp.dot(act(0, block), w_out[:, cols], preferred_element_type=jnp.float32)
            else:
                value = contract_cols(act(1, block), w_in[0, cols])
                value = value + contract_cols(act(2, block), w_in[1, cols])
                value = value + contract_cols(act(3, block), w_in[2, cols])
            parts[phase, block, :, cols] = value.astype(jnp.bfloat16)
            return carry

        lax.fori_loop(0, features // wide, tile, 0)

    order = []
    for k in range(n_z // 2):
        order += [n_z - 1 - k, k]

    def start_phase(phase):
        for block in order:
            def send(i, carry):
                to = lax.rem(x + i, n_x)
                multiply(phase, block * n_x + to)
                x_copy(phase, block, to, x).start()
                return carry

            lax.fori_loop(1, n_x, send, 0)
            multiply(phase, block * n_x + x)

    def x_total(phase, block):
        value = parts[phase, block * n_x + x].astype(jnp.float32)
        for i in range(1, n_x):
            source = lax.rem(x + i, n_x)
            x_copy(phase, block, x, source).wait_recv()
            value = value + x_got[phase, source, block].astype(jnp.float32)
        parts[phase, block * n_x + x] = value.astype(jnp.bfloat16)

    def add_z(phase, block, way):
        z_copy(phase, block, way).wait_recv()
        slot = block * n_x + x
        parts[phase, slot] = (
            parts[phase, slot].astype(jnp.float32) + z_got[phase, way, block].astype(jnp.float32)
        ).astype(jnp.bfloat16)

    def reduce_step(phase, block):
        x_total(phase, block)

        @pl.when(z < block)
        def _():
            @pl.when(z > 0)
            def _():
                add_z(phase, block, 0)

            z_copy(phase, block, 0).start()

        @pl.when(z > block)
        def _():
            @pl.when(z + 1 < n_z)
            def _():
                add_z(phase, block, 1)

            z_copy(phase, block, 1).start()

    def final(phase, out):
        @pl.when(z > 0)
        def _():
            add_z(phase, z, 0)

        @pl.when(z + 1 < n_z)
        def _():
            add_z(phase, z, 1)

        out[...] = parts[phase, z * n_x + x]

    pass_on(0)
    weight_copies[0].wait()
    settle(0)
    start_phase(0)
    for k, block in enumerate(order):
        if k < 3:
            pass_on(k + 1)
        reduce_step(0, block)
    for m in range(1, 4):
        settle(m)
        weight_copies[m].wait()
    start_phase(1)
    final(0, block_out)
    for block in order:
        reduce_step(1, block)
    final(1, tokens_grad)

    for m in range(4):
        for i in range(1, n_y):
            g_copy(m, me, i, partner).wait_send()
            g_copy(m, me, n_y - 1 + i, partner).wait_send()
        g_copy(m, me, 0, partner).wait_send()
        for source in range(n_row):
            out_copy(m, source).wait()
    for phase in range(2):
        def finish(block, carry):
            for i in range(1, n_x):
                x_copy(phase, block, lax.rem(x + i, n_x), x).wait_send()

            @pl.when(z != block)
            def _():
                z_copy(phase, block, 0).wait_send()

            return carry

        lax.fori_loop(0, n_z, finish, 0)


def shift_down(value, by):
    return jnp.pad(value, ((by, 0), (0, 0)))[: value.shape[0]] if by else value


def shift_up(value, by):
    return jnp.pad(value, ((0, by), (0, 0)))[by:] if by else value


def local(tokens, query_weight, key_weight, value_weight, out_weight, filter_taps, out_grad):
    n_row, n_col = lax.axis_size("row"), lax.axis_size("col")
    me = lax.axis_index("row")
    n_z, n_x, n_y = Z_LINE, n_col // Z_LINE, n_row // CORES
    block_rows, features = tokens.shape
    hidden = query_weight.shape[1]
    total_tokens = block_rows * n_col
    slice_cols = hidden // n_row
    bf16 = jnp.bfloat16
    anywhere = pl.BlockSpec(memory_space=pl.ANY)
    inside = pl.BlockSpec(memory_space=pltpu.VMEM)
    dma = pltpu.SemaphoreType.DMA
    gathered = jax.ShapeDtypeStruct((n_col, block_rows, features), bf16)
    sums, full_tokens, full_grads = pl.pallas_call(
        functools.partial(forward_kernel, n_col, n_row, n_z),
        out_shape=(
            jax.ShapeDtypeStruct((4, n_col, block_rows, slice_cols), bf16), gathered, gathered,
        ),
        in_specs=[anywhere] * 6,
        out_specs=(inside, anywhere, anywhere),
        scratch_shapes=[
            pltpu.VMEM((2, n_col, block_rows, features), bf16),
            pltpu.VMEM((3, features, hidden), bf16),
            pltpu.VMEM((hidden, features), bf16),
            pltpu.VMEM((n_row, n_col, 4, block_rows, slice_cols), bf16),
            pltpu.VMEM((n_row, n_col, 4, block_rows, slice_cols), bf16),
            dma((2, 2, n_z)), dma((2, n_z)),
            dma((2, n_z, n_x)), dma((2, n_z, n_x)),
            dma((2, n_row, n_col)), dma((2, n_row, n_col)),
            dma((4,)), dma((2,)), dma((2, n_col)),
        ],
        compiler_params=pltpu.CompilerParams(
            collective_id=0, has_side_effects=True, vmem_limit_bytes=VMEM_BYTES
        ),
        name="gather_project",
    )(tokens, out_grad, query_weight, key_weight, value_weight, out_weight)
    full_tokens = full_tokens.reshape(total_tokens, features)
    full_grads = full_grads.reshape(total_tokens, features)
    query, keys, values, gated_grad = [
        sums[m].reshape(total_tokens, slice_cols).astype(jnp.float32) for m in range(4)
    ]
    own_groups = slice_cols // GROUP
    taps = lax.dynamic_slice_in_dim(filter_taps, me * own_groups, own_groups, axis=1)
    taps = jnp.repeat(taps, GROUP, axis=1)
    product = (keys * values).astype(bf16).astype(jnp.float32)
    conv_out = sum(taps[j][None, :] * shift_down(product, j) for j in range(KW))
    conv_out = conv_out.astype(bf16).astype(jnp.float32)
    gated = (query * conv_out).astype(bf16)
    query_back = (gated_grad * conv_out).astype(bf16)
    conv_grad = (gated_grad * query).astype(bf16).astype(jnp.float32)
    product_grad = sum(taps[j][None, :] * shift_up(conv_grad, j) for j in range(KW))
    keys_back = (product_grad * values).astype(bf16)
    values_back = (product_grad * keys).astype(bf16)
    taps_rows = jnp.stack(
        [jnp.sum(conv_grad * shift_down(product, j), axis=0) for j in range(KW)]
    )
    taps_own = taps_rows.reshape(KW, own_groups, GROUP).sum(axis=2)
    taps_grad = lax.all_gather(taps_own, "row", axis=1, tiled=True)
    acts = jnp.stack([gated, query_back, keys_back, values_back])
    shard = jax.ShapeDtypeStruct((block_rows, features), bf16)
    block_out, tokens_grad, acts_all = pl.pallas_call(
        functools.partial(backward_kernel, n_col, n_row, n_z),
        out_shape=(
            shard, shard, jax.ShapeDtypeStruct((4, n_row, total_tokens, slice_cols), bf16),
        ),
        in_specs=[anywhere] * 5,
        out_specs=(inside, inside, anywhere),
        scratch_shapes=[
            pltpu.VMEM((4, n_row, total_tokens, slice_cols), bf16),
            pltpu.VMEM((hidden, features), bf16),
            pltpu.VMEM((3, features, hidden), bf16),
            pltpu.VMEM((2, n_col, block_rows, features), bf16),
            pltpu.VMEM((2, n_x, n_z, block_rows, features), bf16),
            pltpu.VMEM((2, 2, n_z, block_rows, features), bf16),
            dma((4,)), dma((4,)),
            dma((4, 2 * n_y)), dma((4, n_row)),
            dma((2, n_z, n_x)), dma((2, n_x, n_z)),
            dma((2, n_z)), dma((2, 2, n_z)),
            dma((4, n_row)),
        ],
        compiler_params=pltpu.CompilerParams(
            collective_id=1, has_side_effects=True, vmem_limit_bytes=VMEM_BYTES
        ),
        name="gather_scatter",
    )(acts, out_weight, query_weight, key_weight, value_weight)
    joined = jnp.transpose(acts_all, (0, 2, 1, 3)).reshape(4, total_tokens, hidden)
    query_grad = contract_rows(full_tokens, joined[1]).astype(bf16)
    key_grad = contract_rows(full_tokens, joined[2]).astype(bf16)
    value_grad = contract_rows(full_tokens, joined[3]).astype(bf16)
    outw_grad = contract_rows(joined[0], full_grads).astype(bf16)
    return (block_out, tokens_grad, query_grad, key_grad, value_grad, outw_grad, taps_grad)


def solution(mesh):
    in_specs = (
        P("col", "row"),
        P("row", "col"),
        P("row", "col"),
        P("row", "col"),
        P("col", "row"),
        P(None, "col"),
        P("col", "row"),
    )
    out_specs = (
        P("col", "row"),
        P("col", "row"),
        P("row", "col"),
        P("row", "col"),
        P("row", "col"),
        P("col", "row"),
        P(None, "col"),
    )
    return jax.shard_map(local, mesh=mesh, in_specs=in_specs, out_specs=out_specs, check_vma=False)
```

time: 559 us -> 380 us (0.68)
  waiting for transfers between devices: 378 us -> 0 us
  Pallas kernels: 0 us -> 295 us
  matrix products: 109 us -> 37.8 us
  between operations: 14.8 us -> 1.24 us
  other arithmetic: 14.9 us -> 7.79 us
    pallas_call x0 -> x2, Pallas kernels: none -> 295 us  [the longest x1 161 us: local(): pl.pallas_call(functools.partial(backward_kernel, n_col, n_row, n_z), out...]
    reduce_scatter x4 -> x0, waiting for transfers between devices: 193 us -> none  [the longest x1 92.3 us: local(): lax.psum_scatter(jnp.dot(rows, out_weight, preferred_element_type=jnp.flo...]
    all_gather x6 -> x0, waiting for transfers between devices: 180 us -> none  [the longest x1 77.6 us: local(): full_tokens = lax.all_gather(tokens, 'col', axis=0, tiled=True)]
    dot_general x6 -> x0, matrix products: 74.9 us -> none  [the longest x4 45.1 us: contract_cols(): lax.dot_general(left, right, (((1,), (1,)), ((), ())), preferred_element_...]
    slice x3 -> x6, local copies, waits for them, and re-layouts: 0.16 us -> 20.3 us  [the longest x2 9.63 us: local(): outw_grad = contract_rows(joined[0], full_grads).astype(bf16)]
    unnamed x19 -> x21, local copies, waits for them, and re-layouts: 19.8 us -> 4.04 us
    convert_element_type x4 -> x5, other arithmetic: 11.1 us -> 3.19 us  [the longest x1 1.76 us: local(): gated = (query * conv_out).astype(bf16)]
    psum x1 -> x0, blocking collectives: 7.16 us -> none  [local(): taps_grad = lax.psum(taps_term, 'row')]
  transfers between devices with their start and end apart: 12 -> 0, of which waited for: 11 -> 0; matrix products, arithmetic and copies ran while one was open for 26% -> 0% of each run, Pallas kernels for 0% -> 0%
where the time goes in v1:
time: 380 us; the launch traced here: 373 us
  Pallas kernels  295 us (78%)
  matrix products  37.8 us (10%)
  local copies, waits for them, and re-layouts  26 us (7%)
  other arithmetic  7.79 us (2%)
  blocking collectives  5.19 us (1%)
    pallas_call x1, Pallas kernels, local(): pl.pallas_call(functools.partial(backward_kernel, n_col, n_row, n_z), out...  161 us
    pallas_call x1, Pallas kernels, local(): pl.pallas_call(functools.partial(forward_kernel, n_col, n_row, n_z), out_...  134 us
    dot_general x4, matrix products, contract_rows(): lax.dot_general(left, right, (((0,), (0,)), ((), ())), preferred_element_...  37.8 us
    slice x2, local copies, waits for them, and re-layouts, local(): outw_grad = contract_rows(joined[0], full_grads).astype(bf16)  9.63 us

profile of v1, /device:TPU:0, one launch (start us, length us, event | category | flops | bytes accessed | tf_op | source)
XLA Modules:
  0.0 372.9 jit_solution(8567050292791800943)
XLA Ops:
  0.7 0.7 copy-done
  2.5 134.1 %gather_project.1 = (bf16[4,8,128,256]{3,2,1,0:T(8,128)(2,1)}, bf16[8,128,2048]{2,1,0:T(8,128)(2,1)}, bf16[8,128,2048]{2,1,0:T(8,128)(2,1)}) custom-call(bf16[128,2048]{1,0:T(8,128)(2,1)} %tokens.1, bf16[128,2048]{1,0:T(8,128)(2,1)} %grads.1, bf16[2048,1024]{1,0:T(8,128)(2,1)} %wq.3, bf16[2048,1024]{1,0:T(8,128)(2,1)} %wk.3, bf16[2048,1024]{1,0:T(8,128)(2,1)} %wv.3, ...), custom_call_target="tpu_custom_call" | custom-call | tf_op jit(solution)/shard_map/gather_project/pallas_call | solution.py:424
  136.6 2.0 multiply_reduce_fusion
  138.6 0.2 copy-done.2
  138.9 1.0 fusion.19
  139.9 1.8 fusion.12
  142.3 5.2 %all-gather = f32[4,16,7]{1,2,0:T(8,128)S(1)} all-gather(f32[1,16,7]{1,2,0:T(8,128)S(1)} %bitcast.74), channel_id=1, replica_groups=mesh['row'=4,'col'=8] {'row'}, dimensions={0}, use_global_device_ids=true | all-gather | bytes 2240 | tf_op jit(solution)/shard_map/all_gather | solution.py:468
  147.4 0.7 reshape.88
  148.2 1.1 fusion.24
  149.3 0.1 fusion.25
  149.5 0.9 copy-done.3
  150.3 1.6 pad_maximum_fusion.acts
  151.9 160.7 %gather_scatter.1 = (bf16[128,2048]{1,0:T(8,128)(2,1)}, bf16[128,2048]{1,0:T(8,128)(2,1)}, bf16[4,4,1024,256]{3,2,1,0:T(8,128)(2,1)}) custom-call(bf16[4,1024,256]{2,1,0:T(8,128)(2,1)} %pad_maximum_fusion.acts, bf16[1024,2048]{1,0:T(8,128)(2,1)} %wo.3, bf16[2048,1024]{1,0:T(8,128)(2,1)} %wq.3, bf16[2048,1024]{1,0:T(8,128)(2,1)} %wk.3, bf16[2048,1024]{1,0:T(8,128)(2,1)} %wv.3), custom_call_target="tpu_custom_call" | custom-call | tf_op jit(solution)/shard_map/gather_scatter/pallas_call | solution.py:471
  312.7 5.7 %fusion.29 = (bf16[1,1024,4,256]{3,1,2,0:T(8,128)(2,1)}, bf16[1,1024,4,256]{3,1,2,0:T(8,128)(2,1)}, bf16[1,1024,4,256]{3,1,2,0:T(8,128)(2,1)}, bf16[1,1024,4,256]{3,1,2,0:T(8,128)(2,1)S(1)}) fusion(bf16[4,1024,4,256]{3,1,2,0:T(8,128)(2,1)} %bitcast.65), kind=kLoop, calls=%fused_computation.76 | loop fusion | bytes 16777216 | tf_op jit(solution)/shard_map/slice | solution.py:500
  318.4 3.9 %copy.27 = bf16[1,1024,4,256]{1,3,2,0:T(8,128)(2,1)} copy(bf16[1,1024,4,256]{3,1,2,0:T(8,128)(2,1)} %get-tuple-element.30) | data formatting | bytes 4194304 | tf_op jit(solution)/shard_map/slice | solution.py:500
  322.3 9.3 %convolution_convert_fusion = bf16[1024,2048]{1,0:T(8,128)(2,1)} fusion(bf16[1024,1024]{0,1:T(8,128)(2,1)} %bitcast.66, bf16[1024,2048]{1,0:T(8,128)(2,1)} %bitcast.79), kind=kOutput, calls=%fused_computation | convolution fusion | flops 4297064448 | bytes 10485760 | tf_op jit(solution)/shard_map/dot_general | solution.py:21
  331.7 3.9 %copy.26 = bf16[1,1024,4,256]{1,3,2,0:T(8,128)(2,1)} copy(bf16[1,1024,4,256]{3,1,2,0:T(8,128)(2,1)} %get-tuple-element.31) | data formatting | bytes 4194304 | tf_op jit(solution)/shard_map/slice | solution.py:499
  335.6 9.5 %convolution_convert_fusion.1 = bf16[2048,1024]{1,0:T(8,128)(2,1)} fusion(bf16[1024,2048]{1,0:T(8,128)(2,1)} %bitcast.76, bf16[1024,1024]{0,1:T(8,128)(2,1)} %bitcast.68), kind=kOutput, calls=%fused_computation.1 | convolution fusion | flops 4297064448 | bytes 10485760 | tf_op jit(solution)/shard_map/dot_general | solution.py:21
  345.1 4.2 %copy.25 = bf16[1,1024,4,256]{1,3,2,0:T(8,128)(2,1)} copy(bf16[1,1024,4,256]{3,1,2,0:T(8,128)(2,1)} %get-tuple-element.32) | data formatting | bytes 4194304 | tf_op jit(solution)/shard_map/slice | solution.py:498
  349.3 9.5 %convolution_convert_fusion.2 = bf16[2048,1024]{1,0:T(8,128)(2,1)} fusion(bf16[1024,2048]{1,0:T(8,128)(2,1)} %bitcast.77, bf16[1024,1024]{0,1:T(8,128)(2,1)} %bitcast.69), kind=kOutput, calls=%fused_computation.2 | convolution fusion | flops 4297064448 | bytes 10485760 | tf_op jit(solution)/shard_map/dot_general | solution.py:21
  358.7 2.5 copy.24
  361.2 9.5 %convolution_convert_fusion.3 = bf16[2048,1024]{1,0:T(8,128)(2,1)} fusion(bf16[1024,2048]{1,0:T(8,128)(2,1)} %bitcast.78, bf16[1024,1024]{0,1:T(8,128)(2,1)} %bitcast.67), kind=kOutput, calls=%fused_computation.3 | convolution fusion | flops 4297064448 | bytes 10485760 | tf_op jit(solution)/shard_map/dot_general | solution.py:21
  370.8 0.8 copy.37
  371.6 0.8 copy.38
  (43 shorter events, 2.0 us)
Async XLA Ops:
  0.6 0.7 copy-start
  136.6 2.2 copy-start.2
  149.3 1.0 copy-start.3
  361.2 9.5 %copy-start.5 = (bf16[128,2048]{1,0:T(8,128)(2,1)S(1)}, bf16[128,2048]{1,0:T(8,128)(2,1)}, u32[]{:S(2)}) copy-start(bf16[128,2048]{1,0:T(8,128)(2,1)} %get-tuple-element.49) | copy-start | bytes 1572868
  361.2 10.3 %copy-start.4 = (bf16[128,2048]{1,0:T(8,128)(2,1)S(1)}, bf16[128,2048]{1,0:T(8,128)(2,1)}, u32[]{:S(2)}) copy-start(bf16[128,2048]{1,0:T(8,128)(2,1)} %get-tuple-element.50) | copy-start | bytes 1572868
  361.2 11.1 %copy-start.1 = (f32[7,64]{1,0:T(8,128)S(1)}, f32[7,64]{1,0:T(8,128)}, u32[]{:S(2)}) copy-start(f32[7,64]{1,0:T(8,128)} %param.12) | copy-start | bytes 5380
